TPU v7x, 32 devices: a whole 2x2x4 slice. The times are simulated.
32 devices in a mesh: row: 4 (over x, core), col: 4 (over z), depth: 2 (over y).
Axes of the slice: x: 2, y: 2, z: 4, core: 2. Of those that a mesh axis runs over, the one named last changes fastest.
Arguments:
- activations: bfloat16 [4096, 4544], P(('depth', 'row'), 'col'), may hold values from -6 to 6
- out_grads: bfloat16 [4096, 12288], P(('depth', 'col'), 'row'), may hold values from -0.125 to 0.125
Outputs:
- weight_grad: float32 [12288, 4544], P(('row', 'depth'), 'col')
All inputs are finite; a program needn't handle non-finite values.
Results may differ from a plain program's by a relative error of at most 0.0003.
Values may be sent and summed in bfloat16 or wider, within the bound.
A program may use at most 128 MiB of HBM per device.

v0:
```python
import jax
import jax.numpy as jnp
from jax import lax
from jax.sharding import PartitionSpec as P


def contract(left, right):
    return lax.dot_general(
        left, right, (((0,), (0,)), ((), ())), preferred_element_type=jnp.float32
    )


def gather_acts(activations):
    return lax.all_gather(activations, "row", axis=0, tiled=True)


def body(activations, out_grads):
    whole_acts = gather_acts(activations)
    partial_tile = contract(lax.all_gather(out_grads, "col", axis=0, tiled=True), whole_acts)
    return lax.psum_scatter(partial_tile, "depth", scatter_dimension=0, tiled=True)


def solution(mesh):
    in_specs = (P(("depth", "row"), "col"), P(("depth", "col"), "row"))
    out_specs = P(("row", "depth"), "col")
    return jax.shard_map(body, mesh=mesh, in_specs=in_specs, out_specs=out_specs, check_vma=False)
```

profile of v0, /device:TPU:0, one launch (start us, length us, event | category | flops | bytes accessed | tf_op | source)
XLA Modules:
  0.0 453.7 jit_solution(3856362138217180752)
XLA Ops:
  6.5 0.0 all-gather.5.cloned.1.call-start
  6.5 0.7 all-gather.5.cloned.1.call-update
  7.3 0.0 all-gather.3.cloned.1.call-start
  7.3 0.7 all-gather.3.cloned.1.call-update
  8.0 0.0 reduce-scatter.2.cloned.1.call-start
  8.1 40.7 %all-gather.5.cloned.1.call-done = bf16[2048,1136]{0,1:T(8,128)(2,1)} async-done(((bf16[512,1136]{0,1:T(8,128)(2,1)}), bf16[2048,1136]{0,1:T(8,128)(2,1)}) %all-gather.5.cloned.1.call-update) | async-done | bytes 4653072 | tf_op jit(solution)/shard_map/all_gather | solution.py:14
  48.7 219.8 %all-gather.3.cloned.1.call-done = bf16[2048,3072]{1,0:T(8,128)(2,1)} async-done(((bf16[512,3072]{1,0:T(8,128)(2,1)}), bf16[2048,3072]{1,0:T(8,128)(2,1)}) %all-gather.3.cloned.1.call-update) | async-done | bytes 12582928 | tf_op jit(solution)/shard_map/all_gather | solution.py:19
  268.5 20.9 %fusion = f32[3072,1136]{0,1:T(8,128)} fusion(bf16[2048,1136]{0,1:T(8,128)(2,1)} %all-gather.5.cloned.1.call-done, bf16[2048,3072]{1,0:T(8,128)(2,1)} %all-gather.3.cloned.1.call-done), kind=kOutput, calls=%fused_computation | convolution fusion | flops 14294188032 | bytes 31195136 | tf_op jit(solution)/shard_map/dot_general | solution.py:8
  289.5 0.0 reduce-scatter.2.cloned.1.call-update
  289.5 157.7 %reduce-scatter.2.cloned.1.call-done = f32[1536,1136]{0,1:T(8,128)} async-done(((f32[3072,1136]{0,1:T(8,128)}), f32[1536,1136]{0,1:T(8,128)}) %reduce-scatter.2.cloned.1.call-update) | async-done | bytes 6979600 | tf_op jit(solution)/shard_map/reduce_scatter | solution.py:20
Async XLA Ops:
  6.5 42.2 %all-gather.5.cloned.1.call-start = ((), (), s32[]{:S(2)}) async-start(), calls=%async_computation.2 | async-start | bytes 5816320 | tf_op jit(solution)/shard_map/all_gather | solution.py:14
  7.3 261.3 %all-gather.3.cloned.1.call-start = ((), (), s32[]{:S(2)}) async-start(), calls=%async_computation.1 | async-start | bytes 15728640 | tf_op jit(solution)/shard_map/all_gather | solution.py:19
  8.0 439.1 %reduce-scatter.2.cloned.1.call-start = ((), (), s32[]{:S(2)}) async-start(), calls=%async_computation.3 | async-start | bytes 20938752 | tf_op jit(solution)/shard_map/reduce_scatter | solution.py:20
Sparse Core Ops, SparseCore 0:
  8.9 39.7 all-gather.4
  50.3 218.2 all-gather.2
  289.6 157.4 reduce-scatter.1
where the time goes:
time: 454 us
  waiting for transfers between devices  420 us (93%)
  matrix products  20.9 us (5%)
  between operations  13.1 us (3%)
    all_gather x1, waiting for transfers between devices, body(): lax.all_gather(out_grads, 'col', axis=0, tiled=True)  220 us
    reduce_scatter x1, waiting for transfers between devices, body(): lax.psum_scatter(partial_tile, 'depth', scatter_dimension=0, tiled=True)  158 us
    all_gather x1, waiting for transfers between devices, gather_acts(): return lax.all_gather(activations, 'row', axis=0, tiled=True)  40.7 us
    dot_general x1, matrix products, contract(): lax.dot_general(left, right, (((0,), (0,)), ((), ())), preferred_element_...  20.9 us
  transfers between devices with their start and end apart: 3, of which 3 were waited for; matrix products, arithmetic and copies ran while one was open for 0% of the time, Pallas kernels for 0%

commit v1 on v0

v1 whole, which is shorter than its diff:
```python
import functools

import jax
import jax.numpy as jnp
from jax import lax
from jax.experimental import pallas as pl
from jax.experimental.pallas import tpu as pltpu
from jax.sharding import PartitionSpec as P

MESH = pl.DeviceIdType.MESH
CHUNKS = 2
TILE = 256


def contract(left, right):
    return lax.dot_general(
        left, right, (((0,), (0,)), ((), ())), preferred_element_type=jnp.float32
    )


def gather_acts(activations):
    return lax.all_gather(activations, "row", axis=0, tiled=True)


def body(activations, out_grads):
    whole_acts = gather_acts(activations)
    partial_tile = contract(lax.all_gather(out_grads, "col", axis=0, tiled=True), whole_acts)
    return lax.psum_scatter(partial_tile, "depth", scatter_dimension=0, tiled=True)


def kernel(
    cols, acts_hbm, grads_hbm, out_ref, acts, grads,
    local_sem, acts_recv, acts_send, grads_recv, send_right, send_left, send_y,
):
    r, z, y = lax.axis_index("row"), lax.axis_index("col"), lax.axis_index("depth")
    tokens = acts_hbm.shape[0]
    half = out_ref.shape[0]
    piece = tokens // CHUNKS
    last = cols - 1
    other_y = 1 - y
    sib = r + 1 - 2 * lax.rem(r, 2)
    across = lax.rem(r + 2, 4)
    across_sib = sib + across - r
    to_sib, to_x, to_y = {"row": sib}, {"row": across}, {"depth": other_y}
    to_right, to_left = {"col": jnp.minimum(z + 1, last)}, {"col": jnp.maximum(z - 1, 0)}

    barrier = pltpu.get_barrier_semaphore()
    for partner in (to_sib, to_x, to_y):
        pl.semaphore_signal(barrier, inc=1, device_id=partner, device_id_type=MESH)

    @pl.when(z < last)
    def _():
        pl.semaphore_signal(barrier, inc=1, device_id=to_right, device_id_type=MESH)

    @pl.when(z > 0)
    def _():
        pl.semaphore_signal(barrier, inc=1, device_id=to_left, device_id_type=MESH)

    pl.semaphore_wait(barrier, 3 + (z < last).astype(jnp.int32) + (z > 0).astype(jnp.int32))

    def rows(c):
        return pl.ds(pl.multiple_of(c * piece, piece), piece)

    mine = pl.ds(pl.multiple_of(y * half, half), half)
    theirs = pl.ds(pl.multiple_of(other_y * half, half), half)

    def remote(src, dst, send, recv, device):
        return pltpu.make_async_remote_copy(
            src_ref=src, dst_ref=dst, send_sem=send, recv_sem=recv,
            device_id=device, device_id_type=MESH,
        )

    def swap(c):
        return remote(
            grads_hbm.at[rows(c), theirs], grads.at[y, z, rows(c)],
            send_y.at[c], grads_recv.at[y, z, c], to_y,
        )

    def own_right(c):
        return remote(
            grads_hbm.at[rows(c), mine], grads.at[y, z, rows(c)],
            send_right.at[y, z, c], grads_recv.at[y, z, c], to_right,
        )

    def own_left(c):
        return remote(
            grads_hbm.at[rows(c), mine], grads.at[y, z, rows(c)],
            send_left.at[y, z, c], grads_recv.at[y, z, c], to_left,
        )

    def on_right(yy, zz, c):
        block = grads.at[yy, zz, rows(c)]
        return remote(block, block, send_right.at[yy, zz, c], grads_recv.at[yy, zz, c], to_right)

    def on_left(yy, zz, c):
        block = grads.at[yy, zz, rows(c)]
        return remote(block, block, send_left.at[yy, zz, c], grads_recv.at[yy, zz, c], to_left)

    def arrived(yy, zz, c):
        block = grads.at[yy, zz, rows(c)]
        pltpu.make_async_copy(block, block, grads_recv.at[yy, zz, c]).wait()

    def acts_copy(src, yy, rr, which, device):
        return remote(src, acts.at[yy, rr], acts_send.at[which], acts_recv.at[yy, rr], device)

    def acts_on(yy, rr, which, device):
        return acts_copy(acts.at[yy, rr], yy, rr, which, device)

    def acts_arrived(yy, rr):
        pltpu.make_async_copy(acts.at[yy, rr], acts.at[yy, rr], acts_recv.at[yy, rr]).wait()

    for c in range(CHUNKS):
        swap(c).start()

        @pl.when(z < last)
        def _():
            own_right(c).start()

        @pl.when(z > 0)
        def _():
            own_left(c).start()

    own_to_x = acts_copy(acts_hbm, y, r, 0, to_x)
    own_to_sib = acts_copy(acts_hbm, y, r, 1, to_sib)
    own_to_y = acts_copy(acts_hbm, y, r, 2, to_y)
    own_to_x.start()
    own_to_sib.start()
    keep_acts = pltpu.make_async_copy(acts_hbm, acts.at[y, r], local_sem.at[0])
    keep_grads = pltpu.make_async_copy(grads_hbm.at[:, mine], grads.at[y, z], local_sem.at[1])
    keep_acts.start()
    keep_grads.start()
    out_ref[...] = jnp.zeros_like(out_ref)

    for c in range(CHUNKS):
        arrived(other_y, z, c)

        @pl.when(z < last)
        def _():
            on_right(other_y, z, c).start()

        @pl.when(z > 0)
        def _():
            on_left(other_y, z, c).start()

    own_to_y.start()
    acts_arrived(y, across)
    x_to_sib = acts_on(y, across, 3, to_sib)
    x_to_sib.start()

    def take(step, yy, c):
        from_left = z - step
        from_right = z + step

        @pl.when(from_left >= 0)
        def _():
            arrived(yy, from_left, c)

            @pl.when(z < last)
            def _():
                on_right(yy, from_left, c).start()

        @pl.when(from_right <= last)
        def _():
            arrived(yy, from_right, c)

            @pl.when(z > 0)
            def _():
                on_left(yy, from_right, c).start()

    def multiply(yy, zz, c):
        tile = TILE if half % TILE == 0 else 128

        @pl.loop(0, half // tile)
        def _(i):
            at = pl.ds(pl.multiple_of(i * tile, tile), tile)
            out_ref[at, :] += contract(grads[yy, zz, rows(c), at], acts[yy, zz, rows(c), :])

    def multiply_both(step, yy, c):
        @pl.when(z - step >= 0)
        def _():
            multiply(yy, z - step, c)

        @pl.when(z + step <= last)
        def _():
            multiply(yy, z + step, c)

    acts_arrived(other_y, r)
    diagonal = acts_on(other_y, r, 4, to_x)
    diagonal.start()
    y_to_sib = acts_on(other_y, r, 5, to_sib)
    y_to_sib.start()
    for c in range(CHUNKS):
        take(1, y, c)
    acts_arrived(other_y, across)
    diagonal_to_sib = acts_on(other_y, across, 6, to_sib)
    diagonal_to_sib.start()
    for c in range(CHUNKS):
        take(1, other_y, c)

    keep_acts.wait()
    keep_grads.wait()
    acts_arrived(y, sib)
    acts_arrived(y, across_sib)
    acts_arrived(other_y, sib)
    acts_arrived(other_y, across_sib)

    @pl.loop(0, 2 * CHUNKS)
    def _(i):
        multiply(i // CHUNKS, z, lax.rem(i, CHUNKS))

    @pl.loop(0, 2 * CHUNKS)
    def _(i):
        multiply_both(1, lax.rem(y + i // CHUNKS, 2), lax.rem(i, CHUNKS))

    @pl.loop(0, (cols - 2) * 2 * CHUNKS)
    def _(i):
        step = 2 + i // (2 * CHUNKS)
        yy = lax.rem(y + lax.rem(i, 2 * CHUNKS) // CHUNKS, 2)
        c = lax.rem(i, CHUNKS)
        take(step, yy, c)
        multiply_both(step, yy, c)

    for copy in (own_to_x, own_to_sib, own_to_y, x_to_sib, diagonal, y_to_sib, diagonal_to_sib):
        copy.wait_send()
    for c in range(CHUNKS):
        swap(c).wait_send()

    @pl.loop(0, cols * 2 * CHUNKS)
    def _(i):
        zz = i // (2 * CHUNKS)
        yy = lax.rem(i, 2 * CHUNKS) // CHUNKS
        c = lax.rem(i, CHUNKS)

        @pl.when((z < last) & (zz <= z))
        def _():
            on_right(yy, zz, c).wait_send()

        @pl.when((z > 0) & (zz >= z))
        def _():
            on_left(yy, zz, c).wait_send()


def fused_body(cols, activations, out_grads):
    tokens, width = activations.shape
    half = out_grads.shape[1] // 2
    dma = pltpu.SemaphoreType.DMA
    return pl.pallas_call(
        functools.partial(kernel, cols),
        out_shape=jax.ShapeDtypeStruct((half, width), jnp.float32),
        in_specs=[pl.BlockSpec(memory_space=pl.ANY)] * 2,
        out_specs=pl.BlockSpec(memory_space=pltpu.VMEM),
        scratch_shapes=[
            pltpu.VMEM((2, cols, tokens, width), jnp.bfloat16),
            pltpu.VMEM((2, cols, tokens, half), jnp.bfloat16),
            dma((2,)),
            dma((2, cols)),
            dma((7,)),
            dma((2, cols, CHUNKS)),
            dma((2, cols, CHUNKS)),
            dma((2, cols, CHUNKS)),
            dma((CHUNKS,)),
        ],
        compiler_params=pltpu.CompilerParams(
            collective_id=0, has_side_effects=True, vmem_limit_bytes=56 * 2**20
        ),
        cost_estimate=pl.CostEstimate(
            flops=2 * half * width * tokens * cols * 2,
            bytes_accessed=4 * half * width + 4 * tokens * (width + 2 * half),
            transcendentals=0,
        ),
    )(activations, out_grads)


def solution(mesh):
    in_specs = (P(("depth", "row"), "col"), P(("depth", "col"), "row"))
    out_specs = P(("row", "depth"), "col")
    rows, cols, depth = mesh.shape["row"], mesh.shape["col"], mesh.shape["depth"]

    def local(activations, out_grads):
        tokens, half = out_grads.shape[0], out_grads.shape[1] // depth
        fits = (rows, cols, depth) == (4, 4, 2) and half % 128 == 0 and tokens % 32 == 0
        if fits:
            return fused_body(cols, activations, out_grads)
        return body(activations, out_grads)

    return jax.shard_map(local, mesh=mesh, in_specs=in_specs, out_specs=out_specs, check_vma=False)
```

time: 454 us -> 224 us (0.49)
  waiting for transfers between devices: 420 us -> 0 us
  Pallas kernels: 0 us -> 214 us
  matrix products: 20.9 us -> 0 us
  between operations: 13.1 us -> 0.01 us
  local copies, waits for them, and re-layouts: 0 us -> 10.4 us
    all_gather x2 -> x0, waiting for transfers between devices: 260 us -> none  [the longest x1 220 us: body(): lax.all_gather(out_grads, 'col', axis=0, tiled=True)]
    pallas_call x0 -> x1, Pallas kernels: none -> 214 us  [fused_body(): pl.pallas_call(functools.partial(kernel, cols), out_shape=jax.ShapeDtypeS...]
    reduce_scatter x1 -> x0, waiting for transfers between devices: 158 us -> none  [body(): lax.psum_scatter(partial_tile, 'depth', scatter_dimension=0, tiled=True)]
    dot_general x1 -> x0, matrix products: 20.9 us -> none  [contract(): lax.dot_general(left, right, (((0,), (0,)), ((), ())), preferred_element_...]
    pallas_call x0 -> x1, local copies, waits for them, and re-layouts: none -> 7.99 us  [fused_body(): pl.pallas_call(functools.partial(kernel, cols), out_shape=jax.ShapeDtypeS...]
  transfers between devices with their start and end apart: 3 -> 0, of which waited for: 3 -> 0; matrix products, arithmetic and copies ran while one was open for 0% -> 0% of each run, Pallas kernels for 0% -> 0%
where the time goes in v1:
time: 224 us
  Pallas kernels  214 us (96%)
  local copies, waits for them, and re-layouts  10.4 us (5%)
    pallas_call x1, Pallas kernels, fused_body(): pl.pallas_call(functools.partial(kernel, cols), out_shape=jax.ShapeDtypeS...  214 us
    pallas_call x1, local copies, waits for them, and re-layouts, fused_body(): pl.pallas_call(functools.partial(kernel, cols), out_shape=jax.ShapeDtypeS...  7.99 us

profile of v1, /device:TPU:0, one launch (start us, length us, event | category | flops | bytes accessed | tf_op | source)
XLA Modules:
  0.0 224.0 jit_solution(3771660735364728660)
XLA Ops:
  0.0 2.4 %copy.3.acts_hbm = bf16[512,1136]{1,0:T(8,128)(2,1)} copy(bf16[512,1136]{0,1:T(8,128)(2,1)} %param.2) | data formatting | bytes 2326528 | tf_op args[0]
  2.4 213.6 %shard_map.28 = f32[1536,1136]{1,0:T(8,128)} custom-call(bf16[512,1136]{1,0:T(8,128)(2,1)} %copy.3.acts_hbm, bf16[512,3072]{1,0:T(8,128)(2,1)} %grads_hbm.1), custom_call_target="tpu_custom_call" | custom-call | flops 14294188032 | bytes 15597568 | tf_op jit(solution)/shard_map/pallas_call | solution.py:247
  216.0 8.0 %copy.4 = f32[1536,1136]{0,1:T(8,128)} copy(f32[1536,1136]{1,0:T(8,128)} %shard_map.28) | data formatting | bytes 13959168 | tf_op jit(solution)/shard_map/pallas_call | solution.py:247

commit v2 on v0

v2 whole, which is shorter than its diff:
```python
import jax
import jax.numpy as jnp
from jax import lax
from jax.experimental import pallas as pl
from jax.experimental.pallas import tpu as pltpu
from jax.sharding import PartitionSpec as P

MESH = pl.DeviceIdType.MESH
PIECES = 6
WHOLE = 3


def contract(left, right):
    return lax.dot_general(
        left, right, (((0,), (0,)), ((), ())), preferred_element_type=jnp.float32
    )


def gather_acts(activations):
    return lax.all_gather(activations, "row", axis=0, tiled=True)


def body(activations, out_grads):
    whole_acts = gather_acts(activations)
    partial_tile = contract(lax.all_gather(out_grads, "col", axis=0, tiled=True), whole_acts)
    return lax.psum_scatter(partial_tile, "depth", scatter_dimension=0, tiled=True)


def kernel(
    acts_hbm, grads_hbm, out_hbm, acts, grads, total, sums,
    local_sem, acts_recv, acts_send, grads_recv, send_mate, send_mid, send_y,
    sums_recv, sums_send, out_sem,
):
    r, z, y = lax.axis_index("row"), lax.axis_index("col"), lax.axis_index("depth")
    wide = total.shape[2]
    half = wide * PIECES
    other_y = 1 - y
    sib = r + 1 - 2 * lax.rem(r, 2)
    across = lax.rem(r + 2, 4)
    across_sib = sib + across - r
    mate = z + 1 - 2 * lax.rem(z, 2)
    opposite = 3 - z
    far = 3 - mate
    helper = (z == 1) | (z == 2)
    to_sib, to_x, to_y, to_mate, to_mid = (
        {"row": sib}, {"row": across}, {"depth": other_y}, {"col": mate}, {"col": opposite}
    )

    barrier = pltpu.get_barrier_semaphore()
    for partner in (to_sib, to_x, to_y, to_mate):
        pl.semaphore_signal(barrier, inc=1, device_id=partner, device_id_type=MESH)

    @pl.when(helper)
    def _():
        pl.semaphore_signal(barrier, inc=1, device_id=to_mid, device_id_type=MESH)

    pl.semaphore_wait(barrier, 4 + helper.astype(jnp.int32))

    def remote(src, dst, send, recv, device):
        return pltpu.make_async_remote_copy(
            src_ref=src, dst_ref=dst, send_sem=send, recv_sem=recv,
            device_id=device, device_id_type=MESH,
        )

    def part(yy, p):
        return pl.ds(pl.multiple_of(yy * half + p * wide, wide), wide)

    def swap(p):
        return remote(
            grads_hbm.at[:, part(other_y, p)], grads.at[y, z, p],
            send_y.at[p], grads_recv.at[y, z, p], to_y,
        )

    def own_mate(p):
        return remote(
            grads_hbm.at[:, part(y, p)], grads.at[y, z, p],
            send_mate.at[y, z, p], grads_recv.at[y, z, p], to_mate,
        )

    def own_mid(p):
        return remote(
            grads_hbm.at[:, part(y, p)], grads.at[y, z, p],
            send_mid.at[y, z, p], grads_recv.at[y, z, p], to_mid,
        )

    def on_mate(yy, zz, p):
        block = grads.at[yy, zz, p]
        return remote(block, block, send_mate.at[yy, zz, p], grads_recv.at[yy, zz, p], to_mate)

    def on_mid(yy, zz, p):
        block = grads.at[yy, zz, p]
        return remote(block, block, send_mid.at[yy, zz, p], grads_recv.at[yy, zz, p], to_mid)

    def arrived(yy, zz, p):
        block = grads.at[yy, zz, p]
        pltpu.make_async_copy(block, block, grads_recv.at[yy, zz, p]).wait()

    def acts_copy(src, of, yy, rr, which, device):
        return remote(src, acts.at[of, yy, rr], acts_send.at[of, which], acts_recv.at[of, yy, rr], device)

    def acts_on(of, yy, rr, which, device):
        return acts_copy(acts.at[of, yy, rr], of, yy, rr, which, device)

    def acts_arrived(of, yy, rr):
        block = acts.at[of, yy, rr]
        pltpu.make_async_copy(block, block, acts_recv.at[of, yy, rr]).wait()

    def own_to_x():
        return acts_copy(acts_hbm, 0, y, r, 0, to_x)

    def own_to_sib():
        return acts_copy(acts_hbm, 0, y, r, 1, to_sib)

    def own_to_y():
        return acts_copy(acts_hbm, 0, y, r, 2, to_y)

    def own_to_helper():
        return acts_copy(acts_hbm, 1, y, r, 7, to_mate)

    def x_to_sib(of):
        return acts_on(of, y, across, 3, to_sib)

    def diagonal(of):
        return acts_on(of, other_y, r, 4, to_x)

    def y_to_sib(of):
        return acts_on(of, other_y, r, 5, to_sib)

    def diagonal_to_sib(of):
        return acts_on(of, other_y, across, 6, to_sib)

    def sib_arrived(of):
        for yy in (y, other_y):
            for rr in (sib, across_sib):
                acts_arrived(of, yy, rr)

    def keep_acts():
        return pltpu.make_async_copy(acts_hbm, acts.at[0, y, r], local_sem.at[PIECES])

    def keep_grads(p):
        return pltpu.make_async_copy(grads_hbm.at[:, part(y, p)], grads.at[y, z, p], local_sem.at[p])

    def product(of, yy, zz, p):
        return jnp.dot(acts[of, yy, zz], grads[yy, zz, p], preferred_element_type=jnp.float32)

    def write(p):
        return pltpu.make_async_copy(
            total.at[p], out_hbm.at[:, pl.ds(pl.multiple_of(p * wide, wide), wide)], out_sem.at[p]
        )

    def send_sum(q):
        return remote(sums.at[q], sums.at[q], sums_send.at[q], sums_recv.at[q], to_mate)

    @pl.when(~helper)
    def _():
        own_to_helper().start()

    for p in range(PIECES):
        swap(p).start()
    own_to_x().start()
    own_to_sib().start()

    @pl.when(~helper)
    def _():
        for p in range(PIECES):
            own_mate(p).start()
            arrived(other_y, z, p)
            on_mate(other_y, z, p).start()
        own_to_y().start()
        keep_acts().start()
        for p in range(PIECES):
            keep_grads(p).start()
        acts_arrived(0, y, across)
        x_to_sib(0).start()
        acts_arrived(0, other_y, r)
        diagonal(0).start()
        y_to_sib(0).start()
        acts_arrived(0, other_y, across)
        diagonal_to_sib(0).start()
        keep_acts().wait()
        for p in range(PIECES):
            keep_grads(p).wait()
        sib_arrived(0)

        @pl.loop(0, PIECES)
        def _(p):
            total[p] = product(0, 0, z, p)
            total[p] += product(0, 1, z, p)

        for zz in (mate, far, opposite):
            @pl.loop(0, WHOLE * 2)
            def _(i):
                p, yy = i // 2, lax.rem(y + i, 2)
                arrived(yy, zz, p)
                total[p] += product(0, yy, zz, p)

        for p in range(WHOLE):
            write(p).start()

        @pl.loop(WHOLE, PIECES)
        def _(p):
            q = p - WHOLE
            pltpu.make_async_copy(sums.at[q], sums.at[q], sums_recv.at[q]).wait()
            total[p] += sums[q]
            write(p).start()

        own_to_helper().wait_send()

        @pl.loop(0, PIECES)
        def _(p):
            own_mate(p).wait_send()
            on_mate(other_y, z, p).wait_send()

    @pl.when(helper)
    def _():
        def own_out(p):
            own_mid(p).start()
            if p < WHOLE:
                own_mate(p).start()
            arrived(other_y, z, p)
            on_mid(other_y, z, p).start()
            if p < WHOLE:
                on_mate(other_y, z, p).start()

        def to_the_end(zz, p):
            for yy in (y, other_y):
                arrived(yy, zz, p)
                if p < WHOLE:
                    on_mate(yy, zz, p).start()

        def to_the_middle(p):
            for yy in (y, other_y):
                arrived(yy, mate, p)
                on_mid(yy, mate, p).start()

        def own_product(p):
            total[p] = product(0, 0, 0, p)

            @pl.loop(1, 8)
            def _(i):
                total[p] += product(0, i // 4, lax.rem(i, 4), p)

            write(p).start()

        def sum_for_end(p):
            q = p - WHOLE
            to_the_end(opposite, p)
            to_the_end(far, p)
            sums[q] = product(1, 0, z, p)
            sums[q] += product(1, 1, z, p)

            @pl.loop(0, 4)
            def _(i):
                zz = jnp.where(i < 2, opposite, far)
                sums[q] += product(1, lax.rem(i, 2), zz, p)

            send_sum(q).start()

        for p in range(WHOLE):
            own_out(p)
        acts_arrived(1, y, r)
        e_to_x = acts_on(1, y, r, 0, to_x)
        e_to_sib = acts_on(1, y, r, 1, to_sib)
        e_to_y = acts_on(1, y, r, 2, to_y)
        e_to_x.start()
        e_to_sib.start()
        e_to_y.start()
        keep_acts().start()
        for p in range(PIECES):
            keep_grads(p).start()
        for p in range(WHOLE):
            to_the_end(opposite, p)
        to_the_middle(0)
        to_the_middle(1)
        own_out(3)
        acts_arrived(1, y, across)
        x_to_sib(1).start()
        acts_arrived(1, other_y, r)
        diagonal(1).start()
        y_to_sib(1).start()
        own_to_y().start()
        acts_arrived(0, y, across)
        x_to_sib(0).start()
        for p in range(2):
            to_the_end(far, p)
        to_the_middle(2)
        to_the_middle(3)
        own_out(4)
        for p in range(2, WHOLE):
            to_the_end(far, p)
        to_the_middle(4)
        own_out(5)
        acts_arrived(1, other_y, across)
        diagonal_to_sib(1).start()
        acts_arrived(0, other_y, r)
        diagonal(0).start()
        y_to_sib(0).start()
        to_the_middle(5)
        for p in range(PIECES):
            keep_grads(p).wait()
        sib_arrived(1)
        sum_for_end(WHOLE)
        acts_arrived(0, other_y, across)
        diagonal_to_sib(0).start()
        keep_acts().wait()
        sib_arrived(0)
        for p in range(WHOLE + 1, PIECES):
            own_product(2 * (p - WHOLE) - 2)
            own_product(2 * (p - WHOLE) - 1)
            sum_for_end(p)
        for p in range(2 * (PIECES - WHOLE) - 2, PIECES):
            own_product(p)

        e_to_x.wait_send()
        e_to_sib.wait_send()
        e_to_y.wait_send()
        x_to_sib(1).wait_send()
        diagonal(1).wait_send()
        y_to_sib(1).wait_send()
        diagonal_to_sib(1).wait_send()

        @pl.loop(0, PIECES)
        def _(p):
            own_mid(p).wait_send()
            on_mid(other_y, z, p).wait_send()
            for yy in range(2):
                on_mid(yy, mate, p).wait_send()

            @pl.when(p < WHOLE)
            def _():
                own_mate(p).wait_send()
                on_mate(other_y, z, p).wait_send()
                for zz in (opposite, far):
                    for yy in range(2):
                        on_mate(yy, zz, p).wait_send()

        for q in range(PIECES - WHOLE):
            send_sum(q).wait_send()

    own_to_x().wait_send()
    own_to_sib().wait_send()
    own_to_y().wait_send()
    x_to_sib(0).wait_send()
    diagonal(0).wait_send()
    y_to_sib(0).wait_send()
    diagonal_to_sib(0).wait_send()

    @pl.loop(0, PIECES)
    def _(p):
        swap(p).wait_send()
        write(p).wait()


def fused_body(activations, out_grads):
    width, tokens = activations.shape
    half = out_grads.shape[1] // 2
    wide = half // PIECES
    dma = pltpu.SemaphoreType.DMA
    return pl.pallas_call(
        kernel,
        out_shape=jax.ShapeDtypeStruct((width, half), jnp.float32),
        in_specs=[pl.BlockSpec(memory_space=pl.ANY)] * 2,
        out_specs=pl.BlockSpec(memory_space=pl.ANY),
        scratch_shapes=[
            pltpu.VMEM((2, 2, 4, width, tokens), jnp.bfloat16),
            pltpu.VMEM((2, 4, PIECES, tokens, wide), jnp.bfloat16),
            pltpu.VMEM((PIECES, width, wide), jnp.float32),
            pltpu.VMEM((PIECES - WHOLE, width, wide), jnp.float32),
            dma((PIECES + 1,)),
            dma((2, 2, 4)),
            dma((2, 8)),
            dma((2, 4, PIECES)),
            dma((2, 4, PIECES)),
            dma((2, 4, PIECES)),
            dma((PIECES,)),
            dma((PIECES - WHOLE,)),
            dma((PIECES - WHOLE,)),
            dma((PIECES,)),
        ],
        compiler_params=pltpu.CompilerParams(
            collective_id=0, has_side_effects=True, vmem_limit_bytes=58 * 2**20
        ),
        cost_estimate=pl.CostEstimate(
            flops=2 * half * width * tokens * 8,
            bytes_accessed=4 * half * width + 4 * tokens * (width + 2 * half),
            transcendentals=0,
        ),
    )(activations, out_grads)


def solution(mesh):
    in_specs = (P(("depth", "row"), "col"), P(("depth", "col"), "row"))
    out_specs = P(("row", "depth"), "col")
    rows, cols, depth = mesh.shape["row"], mesh.shape["col"], mesh.shape["depth"]

    def local(activations, out_grads):
        tokens, half = out_grads.shape[0], out_grads.shape[1] // depth
        fits = (rows, cols, depth) == (4, 4, 2) and half % (128 * PIECES) == 0 and tokens % 128 == 0
        if fits:
            return fused_body(activations.T, out_grads).T
        return body(activations, out_grads)

    return jax.shard_map(local, mesh=mesh, in_specs=in_specs, out_specs=out_specs, check_vma=False)
```

time: 454 us -> 192 us (0.42)
  waiting for transfers between devices: 420 us -> 0 us
  Pallas kernels: 0 us -> 185 us
  matrix products: 20.9 us -> 0 us
  between operations: 13.1 us -> 0.01 us
  local copies, waits for them, and re-layouts: 0 us -> 6.44 us
    all_gather x2 -> x0, waiting for transfers between devices: 260 us -> none  [the longest x1 220 us: body(): lax.all_gather(out_grads, 'col', axis=0, tiled=True)]
    pallas_call x0 -> x1, Pallas kernels: none -> 185 us  [fused_body(): pl.pallas_call(kernel, out_shape=jax.ShapeDtypeStruct((width, half), jnp....]
    reduce_scatter x1 -> x0, waiting for transfers between devices: 158 us -> none  [body(): lax.psum_scatter(partial_tile, 'depth', scatter_dimension=0, tiled=True)]
    dot_general x1 -> x0, matrix products: 20.9 us -> none  [contract(): lax.dot_general(left, right, (((0,), (0,)), ((), ())), preferred_element_...]
    unnamed x0 -> x1, local copies, waits for them, and re-layouts: none -> 6.44 us
  transfers between devices with their start and end apart: 3 -> 0, of which waited for: 3 -> 0; matrix products, arithmetic and copies ran while one was open for 0% -> 0% of each run, Pallas kernels for 0% -> 0%
where the time goes in v2:
time: 192 us
  Pallas kernels  185 us (96%)
  local copies, waits for them, and re-layouts  6.44 us (3%)
    pallas_call x1, Pallas kernels, fused_body(): pl.pallas_call(kernel, out_shape=jax.ShapeDtypeStruct((width, half), jnp....  185 us
    unnamed x1, local copies, waits for them, and re-layouts  6.44 us

profile of v2, /device:TPU:0, one launch (start us, length us, event | category | flops | bytes accessed | tf_op | source)
XLA Modules:
  0.0 191.9 jit_solution(10594875405747796575)
XLA Ops:
  0.0 185.4 %shard_map.28 = f32[1136,1536]{1,0:T(8,128)} custom-call(bf16[1136,512]{1,0:T(8,128)(2,1)} %bitcast.3, bf16[512,3072]{1,0:T(8,128)(2,1)} %grads_hbm.1), custom_call_target="tpu_custom_call" | custom-call | flops 14294188032 | bytes 15597568 | tf_op jit(solution)/shard_map/pallas_call | solution.py:359
  185.4 6.4 %copy.4 = f32[1536,1136]{0,1:T(8,128)} copy(f32[1536,1136]{0,1:T(8,128)} %bitcast.2) | data formatting | bytes 13959168

commit v3 on v2

--- a/solution.py
+++ b/solution.py
@@ -7,7 +7,8 @@
 
 MESH = pl.DeviceIdType.MESH
 PIECES = 6
-WHOLE = 3
+WHOLE = 2
+HALVES = 2
 
 
 def contract(left, right):
@@ -95,27 +96,43 @@
         block = grads.at[yy, zz, p]
         pltpu.make_async_copy(block, block, grads_recv.at[yy, zz, p]).wait()
 
-    def acts_copy(src, of, yy, rr, which, device):
-        return remote(src, acts.at[of, yy, rr], acts_send.at[of, which], acts_recv.at[of, yy, rr], device)
+    def tokens(h):
+        return pl.ds(h * (acts.shape[4] // HALVES), acts.shape[4] // HALVES)
+
+    class Halves:
+        def __init__(self, src, of, yy, rr, which, device):
+            self.copy = lambda h: remote(
+                src.at[:, tokens(h)], acts.at[of, yy, rr, :, tokens(h)],
+                acts_send.at[of, which, h], acts_recv.at[of, yy, rr, h], device,
+            )
+
+        def start(self, halves=range(HALVES)):
+            for h in halves:
+                self.copy(h).start()
+
+        def wait_send(self):
+            for h in range(HALVES):
+                self.copy(h).wait_send()
 
     def acts_on(of, yy, rr, which, device):
-        return acts_copy(acts.at[of, yy, rr], of, yy, rr, which, device)
-
-    def acts_arrived(of, yy, rr):
-        block = acts.at[of, yy, rr]
-        pltpu.make_async_copy(block, block, acts_recv.at[of, yy, rr]).wait()
+        return Halves(acts.at[of, yy, rr], of, yy, rr, which, device)
+
+    def acts_arrived(of, yy, rr, halves=range(HALVES)):
+        for h in halves:
+            block = acts.at[of, yy, rr, :, tokens(h)]
+            pltpu.make_async_copy(block, block, acts_recv.at[of, yy, rr, h]).wait()
 
     def own_to_x():
-        return acts_copy(acts_hbm, 0, y, r, 0, to_x)
+        return Halves(acts_hbm, 0, y, r, 0, to_x)
 
     def own_to_sib():
-        return acts_copy(acts_hbm, 0, y, r, 1, to_sib)
+        return Halves(acts_hbm, 0, y, r, 1, to_sib)
 
     def own_to_y():
-        return acts_copy(acts_hbm, 0, y, r, 2, to_y)
+        return Halves(acts_hbm, 0, y, r, 2, to_y)
 
     def own_to_helper():
-        return acts_copy(acts_hbm, 1, y, r, 7, to_mate)
+        return Halves(acts_hbm, 1, y, r, 7, to_mate)
 
     def x_to_sib(of):
         return acts_on(of, y, across, 3, to_sib)
@@ -155,13 +172,15 @@
     def _():
         own_to_helper().start()
 
-    for p in range(PIECES):
+    for p in range(PIECES // 2):
         swap(p).start()
-    own_to_x().start()
     own_to_sib().start()
 
     @pl.when(~helper)
     def _():
+        for p in range(PIECES // 2, PIECES):
+            swap(p).start()
+        own_to_x().start()
         for p in range(PIECES):
             own_mate(p).start()
             arrived(other_y, z, p)
@@ -245,71 +264,81 @@
         def sum_for_end(p):
             q = p - WHOLE
             to_the_end(opposite, p)
-            to_the_end(far, p)
             sums[q] = product(1, 0, z, p)
             sums[q] += product(1, 1, z, p)
 
-            @pl.loop(0, 4)
-            def _(i):
-                zz = jnp.where(i < 2, opposite, far)
-                sums[q] += product(1, lax.rem(i, 2), zz, p)
+            @pl.loop(0, 2)
+            def _(yy):
+                sums[q] += product(1, yy, opposite, p)
+
+            to_the_end(far, p)
+
+            @pl.loop(0, 2)
+            def _(yy):
+                sums[q] += product(1, yy, far, p)
 
             send_sum(q).start()
 
-        for p in range(WHOLE):
-            own_out(p)
-        acts_arrived(1, y, r)
         e_to_x = acts_on(1, y, r, 0, to_x)
         e_to_sib = acts_on(1, y, r, 1, to_sib)
         e_to_y = acts_on(1, y, r, 2, to_y)
-        e_to_x.start()
-        e_to_sib.start()
-        e_to_y.start()
+        own_out(0)
+        own_out(1)
+        for h in range(HALVES):
+            acts_arrived(1, y, r, (h,))
+            e_to_x.start((h,))
+            e_to_y.start((h,))
+            e_to_sib.start((h,))
+            if h == 0:
+                own_out(2)
+        for p in range(PIECES // 2, PIECES):
+            swap(p).start()
         keep_acts().start()
         for p in range(PIECES):
             keep_grads(p).start()
         for p in range(WHOLE):
             to_the_end(opposite, p)
-        to_the_middle(0)
-        to_the_middle(1)
+        for h in range(HALVES):
+            acts_arrived(1, y, across, (h,))
+            x_to_sib(1).start((h,))
+            acts_arrived(1, other_y, r, (h,))
+            diagonal(1).start((h,))
+            y_to_sib(1).start((h,))
+            to_the_middle(h)
+        own_to_x().start()
+        own_to_y().start()
+        to_the_end(far, 0)
+        to_the_middle(2)
         own_out(3)
-        acts_arrived(1, y, across)
-        x_to_sib(1).start()
-        acts_arrived(1, other_y, r)
-        diagonal(1).start()
-        y_to_sib(1).start()
-        own_to_y().start()
-        acts_arrived(0, y, across)
-        x_to_sib(0).start()
-        for p in range(2):
-            to_the_end(far, p)
-        to_the_middle(2)
+        to_the_end(far, 1)
+        acts_arrived(1, other_y, across)
+        diagonal_to_sib(1).start()
         to_the_middle(3)
         own_out(4)
-        for p in range(2, WHOLE):
-            to_the_end(far, p)
+        for p in range(PIECES):
+            keep_grads(p).wait()
+        sib_arrived(1)
+        sum_for_end(2)
         to_the_middle(4)
         own_out(5)
-        acts_arrived(1, other_y, across)
-        diagonal_to_sib(1).start()
         acts_arrived(0, other_y, r)
         diagonal(0).start()
         y_to_sib(0).start()
+        acts_arrived(0, y, across)
+        x_to_sib(0).start()
         to_the_middle(5)
-        for p in range(PIECES):
-            keep_grads(p).wait()
-        sib_arrived(1)
-        sum_for_end(WHOLE)
+        sum_for_end(3)
         acts_arrived(0, other_y, across)
         diagonal_to_sib(0).start()
         keep_acts().wait()
         sib_arrived(0)
-        for p in range(WHOLE + 1, PIECES):
-            own_product(2 * (p - WHOLE) - 2)
-            own_product(2 * (p - WHOLE) - 1)
-            sum_for_end(p)
-        for p in range(2 * (PIECES - WHOLE) - 2, PIECES):
+        own_product(0)
+        own_product(1)
+        sum_for_end(4)
+        for p in range(2, 5):
             own_product(p)
+        sum_for_end(5)
+        own_product(5)
 
         e_to_x.wait_send()
         e_to_sib.wait_send()
@@ -358,8 +387,8 @@
     dma = pltpu.SemaphoreType.DMA
     return pl.pallas_call(
         kernel,
-        out_shape=jax.ShapeDtypeStruct((width, half), jnp.float32),
-        in_specs=[pl.BlockSpec(memory_space=pl.ANY)] * 2,
+        out_shape=pltpu.VMEM((width, half), jnp.float32),
+        in_specs=[pl.BlockSpec(memory_space=pltpu.HBM)] * 2,
         out_specs=pl.BlockSpec(memory_space=pl.ANY),
         scratch_shapes=[
             pltpu.VMEM((2, 2, 4, width, tokens), jnp.bfloat16),
@@ -367,8 +396,8 @@
             pltpu.VMEM((PIECES, width, wide), jnp.float32),
             pltpu.VMEM((PIECES - WHOLE, width, wide), jnp.float32),
             dma((PIECES + 1,)),
-            dma((2, 2, 4)),
-            dma((2, 8)),
+            dma((2, 2, 4, HALVES)),
+            dma((2, 8, HALVES)),
             dma((2, 4, PIECES)),
             dma((2, 4, PIECES)),
             dma((2, 4, PIECES)),
@@ -378,14 +407,14 @@
             dma((PIECES,)),
         ],
         compiler_params=pltpu.CompilerParams(
-            collective_id=0, has_side_effects=True, vmem_limit_bytes=58 * 2**20
+            collective_id=0, has_side_effects=True, vmem_limit_bytes=44 * 2**20
         ),
         cost_estimate=pl.CostEstimate(
             flops=2 * half * width * tokens * 8,
             bytes_accessed=4 * half * width + 4 * tokens * (width + 2 * half),
             transcendentals=0,
         ),
-    )(activations, out_grads)
+    )(*(pltpu.with_memory_space_constraint(x, pltpu.HBM) for x in (activations, out_grads)))
 
 
 def solution(mesh):
@@ -395,7 +424,7 @@
 
     def local(activations, out_grads):
         tokens, half = out_grads.shape[0], out_grads.shape[1] // depth
-        fits = (rows, cols, depth) == (4, 4, 2) and half % (128 * PIECES) == 0 and tokens % 128 == 0
+        fits = (rows, cols, depth) == (4, 4, 2) and half % (128 * PIECES) == 0 and tokens % (128 * HALVES) == 0
         if fits:
             return fused_body(activations.T, out_grads).T
         return body(activations, out_grads)

time: 192 us -> 186 us (0.969)
  Pallas kernels: 185 us -> 181 us
  local copies, waits for them, and re-layouts: 6.44 us -> 2.93 us
    pallas_call x1, Pallas kernels: 185 us -> 181 us  [fused_body(): pl.pallas_call(kernel, out_shape=pltpu.VMEM((width, half), jnp.float32),...]
    unnamed x1, local copies, waits for them, and re-layouts: 6.44 us -> 2.93 us
where the time goes in v3:
time: 186 us; the launch traced here: 184 us
  Pallas kernels  181 us (97%)
  local copies, waits for them, and re-layouts  2.93 us (2%)
    pallas_call x1, Pallas kernels, fused_body(): pl.pallas_call(kernel, out_shape=pltpu.VMEM((width, half), jnp.float32),...  181 us

profile of v3, /device:TPU:0, one launch (start us, length us, event | category | flops | bytes accessed | tf_op | source)
XLA Modules:
  0.0 184.4 jit_solution(8790438231645923549)
XLA Ops:
  0.0 181.4 %shard_map.28 = f32[1136,1536]{1,0:T(8,128)S(1)} custom-call(bf16[1136,512]{1,0:T(8,128)(2,1)} %bitcast.3, bf16[512,3072]{1,0:T(8,128)(2,1)} %grads_hbm.1), custom_call_target="tpu_custom_call" | custom-call | flops 14294188032 | bytes 15597568 | tf_op jit(solution)/shard_map/pallas_call | solution.py:388
  181.4 2.9 %copy.4 = f32[1536,1136]{0,1:T(8,128)} copy(f32[1536,1136]{0,1:T(8,128)S(1)} %bitcast.2) | data formatting | bytes 13959168

commit v4 on v3

--- a/solution.py
+++ b/solution.py
@@ -137,8 +137,11 @@
     def x_to_sib(of):
         return acts_on(of, y, across, 3, to_sib)
 
-    def diagonal(of):
-        return acts_on(of, other_y, r, 4, to_x)
+    def diagonal_x(of):
+        return acts_on(of, other_y, r, 4, to_x).copy(0)
+
+    def diagonal_y(of):
+        return acts_on(of, y, across, 4, to_y).copy(1)
 
     def y_to_sib(of):
         return acts_on(of, other_y, r, 5, to_sib)
@@ -191,8 +194,9 @@
             keep_grads(p).start()
         acts_arrived(0, y, across)
         x_to_sib(0).start()
+        diagonal_y(0).start()
         acts_arrived(0, other_y, r)
-        diagonal(0).start()
+        diagonal_x(0).start()
         y_to_sib(0).start()
         acts_arrived(0, other_y, across)
         diagonal_to_sib(0).start()
@@ -291,51 +295,56 @@
             e_to_sib.start((h,))
             if h == 0:
                 own_out(2)
-        for p in range(PIECES // 2, PIECES):
-            swap(p).start()
         keep_acts().start()
         for p in range(PIECES):
             keep_grads(p).start()
         for p in range(WHOLE):
             to_the_end(opposite, p)
-        for h in range(HALVES):
-            acts_arrived(1, y, across, (h,))
-            x_to_sib(1).start((h,))
-            acts_arrived(1, other_y, r, (h,))
-            diagonal(1).start((h,))
-            y_to_sib(1).start((h,))
-            to_the_middle(h)
+        acts_arrived(1, y, across, (0,))
+        x_to_sib(1).start((0,))
+        acts_arrived(1, other_y, r, (0,))
+        diagonal_x(1).start()
+        y_to_sib(1).start((0,))
+        to_the_middle(0)
+        acts_arrived(1, y, across, (1,))
+        diagonal_y(1).start()
+        x_to_sib(1).start((1,))
+        acts_arrived(1, other_y, r, (1,))
+        y_to_sib(1).start((1,))
+        for p in range(PIECES // 2, PIECES):
+            swap(p).start()
         own_to_x().start()
         own_to_y().start()
         to_the_end(far, 0)
+        to_the_middle(1)
+        for h in range(HALVES):
+            acts_arrived(1, other_y, across, (h,))
+            diagonal_to_sib(1).start((h,))
+        to_the_end(far, 1)
         to_the_middle(2)
         own_out(3)
-        to_the_end(far, 1)
-        acts_arrived(1, other_y, across)
-        diagonal_to_sib(1).start()
-        to_the_middle(3)
-        own_out(4)
         for p in range(PIECES):
             keep_grads(p).wait()
         sib_arrived(1)
         sum_for_end(2)
+        to_the_middle(3)
+        own_out(4)
         to_the_middle(4)
+        sum_for_end(3)
         own_out(5)
+        to_the_middle(5)
+        acts_arrived(0, y, across)
+        diagonal_y(0).start()
+        x_to_sib(0).start()
         acts_arrived(0, other_y, r)
-        diagonal(0).start()
+        diagonal_x(0).start()
         y_to_sib(0).start()
-        acts_arrived(0, y, across)
-        x_to_sib(0).start()
-        to_the_middle(5)
-        sum_for_end(3)
         acts_arrived(0, other_y, across)
         diagonal_to_sib(0).start()
         keep_acts().wait()
         sib_arrived(0)
-        own_product(0)
-        own_product(1)
         sum_for_end(4)
-        for p in range(2, 5):
+        for p in range(5):
             own_product(p)
         sum_for_end(5)
         own_product(5)
@@ -344,7 +353,8 @@
         e_to_sib.wait_send()
         e_to_y.wait_send()
         x_to_sib(1).wait_send()
-        diagonal(1).wait_send()
+        diagonal_x(1).wait_send()
+        diagonal_y(1).wait_send()
         y_to_sib(1).wait_send()
         diagonal_to_sib(1).wait_send()
 
@@ -370,7 +380,8 @@
     own_to_sib().wait_send()
     own_to_y().wait_send()
     x_to_sib(0).wait_send()
-    diagonal(0).wait_send()
+    diagonal_x(0).wait_send()
+    diagonal_y(0).wait_send()
     y_to_sib(0).wait_send()
     diagonal_to_sib(0).wait_send()
 

time: 186 us -> 181 us (0.973)
  Pallas kernels: 181 us -> 178 us
    pallas_call x1, Pallas kernels: 181 us -> 178 us  [fused_body(): pl.pallas_call(kernel, out_shape=pltpu.VMEM((width, half), jnp.float32),...]
where the time goes in v4:
time: 181 us
  Pallas kernels  178 us (98%)
  local copies, waits for them, and re-layouts  2.93 us (2%)
    pallas_call x1, Pallas kernels, fused_body(): pl.pallas_call(kernel, out_shape=pltpu.VMEM((width, half), jnp.float32),...  178 us

profile of v4, /device:TPU:0, one launch (start us, length us, event | category | flops | bytes accessed | tf_op | source)
XLA Modules:
  0.0 180.5 jit_solution(13335574143804601962)
XLA Ops:
  0.0 177.6 %shard_map.28 = f32[1136,1536]{1,0:T(8,128)S(1)} custom-call(bf16[1136,512]{1,0:T(8,128)(2,1)} %bitcast.3, bf16[512,3072]{1,0:T(8,128)(2,1)} %grads_hbm.1), custom_call_target="tpu_custom_call" | custom-call | flops 14294188032 | bytes 15597568 | tf_op jit(solution)/shard_map/pallas_call | solution.py:399
  177.6 2.9 %copy.4 = f32[1536,1136]{0,1:T(8,128)} copy(f32[1536,1136]{0,1:T(8,128)S(1)} %bitcast.2) | data formatting | bytes 13959168

commit v5 on v4

--- a/solution.py
+++ b/solution.py
@@ -28,12 +28,12 @@
 
 
 def kernel(
-    acts_hbm, grads_hbm, out_hbm, acts, grads, total, sums,
+    acts_hbm, grads_hbm, out_ref, acts, grads, sums,
     local_sem, acts_recv, acts_send, grads_recv, send_mate, send_mid, send_y,
-    sums_recv, sums_send, out_sem,
+    sums_recv, sums_send,
 ):
     r, z, y = lax.axis_index("row"), lax.axis_index("col"), lax.axis_index("depth")
-    wide = total.shape[2]
+    wide = sums.shape[2]
     half = wide * PIECES
     other_y = 1 - y
     sib = r + 1 - 2 * lax.rem(r, 2)
@@ -163,10 +163,8 @@
     def product(of, yy, zz, p):
         return jnp.dot(acts[of, yy, zz], grads[yy, zz, p], preferred_element_type=jnp.float32)
 
-    def write(p):
-        return pltpu.make_async_copy(
-            total.at[p], out_hbm.at[:, pl.ds(pl.multiple_of(p * wide, wide), wide)], out_sem.at[p]
-        )
+    def column(p):
+        return pl.ds(pl.multiple_of(p * wide, wide), wide)
 
     def send_sum(q):
         return remote(sums.at[q], sums.at[q], sums_send.at[q], sums_recv.at[q], to_mate)
@@ -207,25 +205,21 @@
 
         @pl.loop(0, PIECES)
         def _(p):
-            total[p] = product(0, 0, z, p)
-            total[p] += product(0, 1, z, p)
+            out_ref[:, column(p)] = product(0, 0, z, p)
+            out_ref[:, column(p)] += product(0, 1, z, p)
 
         for zz in (mate, far, opposite):
             @pl.loop(0, WHOLE * 2)
             def _(i):
                 p, yy = i // 2, lax.rem(y + i, 2)
                 arrived(yy, zz, p)
-                total[p] += product(0, yy, zz, p)
-
-        for p in range(WHOLE):
-            write(p).start()
+                out_ref[:, column(p)] += product(0, yy, zz, p)
 
         @pl.loop(WHOLE, PIECES)
         def _(p):
             q = p - WHOLE
             pltpu.make_async_copy(sums.at[q], sums.at[q], sums_recv.at[q]).wait()
-            total[p] += sums[q]
-            write(p).start()
+            out_ref[:, column(p)] += sums[q]
 
         own_to_helper().wait_send()
 
@@ -257,13 +251,12 @@
                 on_mid(yy, mate, p).start()
 
         def own_product(p):
-            total[p] = product(0, 0, 0, p)
+            out_ref[:, column(p)] = product(0, 0, 0, p)
 
             @pl.loop(1, 8)
             def _(i):
-                total[p] += product(0, i // 4, lax.rem(i, 4), p)
-
-            write(p).start()
+                out_ref[:, column(p)] += product(0, i // 4, lax.rem(i, 4), p)
+
 
         def sum_for_end(p):
             q = p - WHOLE
@@ -388,7 +381,6 @@
     @pl.loop(0, PIECES)
     def _(p):
         swap(p).wait_send()
-        write(p).wait()
 
 
 def fused_body(activations, out_grads):
@@ -400,11 +392,10 @@
         kernel,
         out_shape=pltpu.VMEM((width, half), jnp.float32),
         in_specs=[pl.BlockSpec(memory_space=pltpu.HBM)] * 2,
-        out_specs=pl.BlockSpec(memory_space=pl.ANY),
+        out_specs=pl.BlockSpec(memory_space=pltpu.VMEM),
         scratch_shapes=[
             pltpu.VMEM((2, 2, 4, width, tokens), jnp.bfloat16),
             pltpu.VMEM((2, 4, PIECES, tokens, wide), jnp.bfloat16),
-            pltpu.VMEM((PIECES, width, wide), jnp.float32),
             pltpu.VMEM((PIECES - WHOLE, width, wide), jnp.float32),
             dma((PIECES + 1,)),
             dma((2, 2, 4, HALVES)),
@@ -415,7 +406,6 @@
             dma((PIECES,)),
             dma((PIECES - WHOLE,)),
             dma((PIECES - WHOLE,)),
-            dma((PIECES,)),
         ],
         compiler_params=pltpu.CompilerParams(
             collective_id=0, has_side_effects=True, vmem_limit_bytes=44 * 2**20

time: 181 us -> 181 us (level)
  no operation moved by 1% of the time
where the time goes in v5:
time: 181 us; the launch traced here: 180 us
  Pallas kernels  177 us (98%)
  local copies, waits for them, and re-layouts  2.93 us (2%)
    pallas_call x1, Pallas kernels, fused_body(): pl.pallas_call(kernel, out_shape=pltpu.VMEM((width, half), jnp.float32),...  177 us

profile of v5, /device:TPU:0, one launch (start us, length us, event | category | flops | bytes accessed | tf_op | source)
XLA Modules:
  0.0 180.4 jit_solution(4701190470935475830)
XLA Ops:
  0.0 177.4 %shard_map.28 = f32[1136,1536]{1,0:T(8,128)S(1)} custom-call(bf16[1136,512]{1,0:T(8,128)(2,1)} %bitcast.3, bf16[512,3072]{1,0:T(8,128)(2,1)} %grads_hbm.1), custom_call_target="tpu_custom_call" | custom-call | flops 14294188032 | bytes 15597568 | tf_op jit(solution)/shard_map/pallas_call | solution.py:391
  177.4 2.9 %copy.4 = f32[1536,1136]{0,1:T(8,128)} copy(f32[1536,1136]{0,1:T(8,128)S(1)} %bitcast.2) | data formatting | bytes 13959168
